TPU v7x, 32 devices: a whole 2x2x4 slice. The times are simulated.
32 devices in a mesh: tensor: 8 (over y, x, core), seq: 4 (over z).
Axes of the slice: x: 2, y: 2, z: 4, core: 2. Of those that a mesh axis runs over, the one named last changes fastest.
Arguments:
- resid: bfloat16 [4, 128, 2048], P('seq', 'tensor'), may hold values from -6 to 6
- norm_gain: bfloat16 [2048], replicated, may hold values from 0.099609375 to 1.8984375
- gate_weight_matrix: bfloat16 [2048, 10944], P(None, 'tensor'), may hold values from -0.125 to 0.125
- up_weight: bfloat16 [2048, 10944], P(None, 'tensor'), may hold values from -0.125 to 0.125
- w_down: bfloat16 [10944, 2048], P('tensor'), may hold values from -0.0546875 to 0.0546875
- gate_a: bfloat16 [16, 2048, 16], P('seq', 'tensor'), may hold values from -0.125 to 0.125
- gate_b: bfloat16 [16, 16, 10944], P('seq', None, 'tensor'), may hold values from -1.5 to 1.5
- up_a: bfloat16 [16, 2048, 16], P('seq', 'tensor'), may hold values from -0.125 to 0.125
- up_b: bfloat16 [16, 16, 10944], P('seq', None, 'tensor'), may hold values from -1.5 to 1.5
- down_a: bfloat16 [16, 10944, 16], P('seq', 'tensor'), may hold values from -0.0546875 to 0.0546875
- down_b: bfloat16 [16, 16, 2048], P('seq'), may hold values from -1.5 to 1.5
- prompt_lengths: int32 [4, 8], P('seq'), may hold values from 1 to 64, 128 in all within a row
- prompt_choice: int32 [4, 8], P('seq'), may hold values from 0 to 15
- used_adapters: int32 [16], replicated, may hold values from 0 to 15, as said below
- adapter_holder: int32 [16], replicated, may hold values from 0 to 15, each once
Outputs:
- output: bfloat16 [4, 128, 2048], P('seq', 'tensor')
Inputs may be any that keep to these rules, and one draw needn't show every extreme that they name: `used_adapters`: 16 distinct adapter ids.
All inputs are finite; a program needn't handle non-finite values.
Results may differ from a plain program's by a relative error of at most 0.017.
Values may be sent and summed in bfloat16 or wider, within the bound.
A program may use at most 128 MiB of HBM per device.

v0:
```python
import jax
import jax.numpy as jnp
from jax import lax
from jax.sharding import PartitionSpec as P

adapter_scale = 0.5


def choose(picker, stacked):
    flat = stacked.reshape(stacked.shape[0], -1)
    chosen = jnp.dot(picker, flat, preferred_element_type=jnp.float32).astype(jnp.bfloat16)
    return chosen.reshape((picker.shape[0],) + stacked.shape[1:])


def to_columns(stacked):
    used_n, inner, rank_n = stacked.shape
    return jnp.transpose(stacked, (1, 0, 2)).reshape(inner, used_n * rank_n)


def local(
    resid,
    norm_gain,
    gate_weight_matrix,
    up_weight,
    w_down,
    gate_a,
    gate_b,
    up_a,
    up_b,
    down_a,
    down_b,
    prompt_lengths,
    prompt_choice,
    used_adapters,
    adapter_holder,
):
    tensor_n = lax.axis_size("tensor")
    tok_dev = resid.shape[1]
    group_tok = tok_dev * tensor_n
    used_n = used_adapters.shape[0]
    rank_n = gate_a.shape[2]
    feat_loc = gate_a.shape[1]
    hidden_local = gate_weight_matrix.shape[1]
    adapters_n = adapter_holder.shape[0]
    matches = used_adapters[:, None] == jnp.arange(adapters_n, dtype=jnp.int32)[None, :]
    slot_used = jnp.sum(jnp.where(matches, adapter_holder[None, :], 0), axis=1)
    whole = (
        lax.all_gather(gate_a, "seq", axis=0, tiled=True),
        lax.all_gather(up_a, "seq", axis=0, tiled=True),
        lax.all_gather(gate_b, "seq", axis=0, tiled=True),
        lax.all_gather(up_b, "seq", axis=0, tiled=True),
        lax.all_gather(down_a, "seq", axis=0, tiled=True),
        lax.all_gather(down_b, "seq", axis=0, tiled=True),
    )
    picker = (slot_used[:, None] == jnp.arange(adapters_n, dtype=jnp.int32)[None, :]).astype(
        jnp.bfloat16
    )
    fetched = tuple((choose(picker, stacked) for stacked in whole))
    fetch_ga, fetch_ua, fetch_gb, fetch_ub, fetch_da, fetch_db = fetched
    prompt_ends = jnp.cumsum(prompt_lengths[0])
    positions = jnp.arange(group_tok, dtype=jnp.int32)
    prompt_index = jnp.sum((positions[:, None] >= prompt_ends[None, :]).astype(jnp.int32), axis=1)
    prompts_n = prompt_lengths.shape[1]
    hits = prompt_index[:, None] == jnp.arange(prompts_n, dtype=jnp.int32)[None, :]
    tok_choice = jnp.sum(jnp.where(hits, prompt_choice[0][None, :], 0), axis=1)
    token_weights = (tok_choice[:, None] == jnp.arange(used_n, dtype=jnp.int32)[None, :]).astype(
        jnp.float32
    )
    row_first = lax.axis_index("tensor") * tok_dev
    own_weights = lax.dynamic_slice_in_dim(token_weights, row_first, tok_dev, 0)
    residual_float = resid[0].astype(jnp.float32)
    scale = lax.rsqrt(jnp.mean(residual_float * residual_float, axis=-1, keepdims=True) + 1e-06)
    normalized_input = (residual_float * scale * norm_gain.astype(jnp.float32)).astype(jnp.bfloat16)
    both_in = jnp.concatenate([to_columns(fetch_ga), to_columns(fetch_ua)], axis=1)
    col_first = lax.axis_index("tensor") * feat_loc
    piece = lax.all_gather(normalized_input, "tensor", axis=0, tiled=True)
    gate_part = jnp.dot(piece, gate_weight_matrix, preferred_element_type=jnp.float32)
    up_part = jnp.dot(piece, up_weight, preferred_element_type=jnp.float32)
    own_cols = lax.dynamic_slice_in_dim(piece, col_first, feat_loc, 1)
    low_part = jnp.dot(own_cols, both_in, preferred_element_type=jnp.float32)
    joined = jnp.concatenate([gate_part, up_part, low_part], axis=1)
    plain_output = joined[:, : 2 * hidden_local]
    low_rank = joined[:, 2 * hidden_local :].reshape(group_tok, 2, used_n, rank_n)
    partial_mid = jnp.sum(low_rank * token_weights[:, None, :, None], axis=2)
    mids = lax.psum(partial_mid.astype(jnp.bfloat16), "tensor")
    weights_bf = token_weights.astype(jnp.bfloat16)
    spread = (mids[:, :, None, :] * weights_bf[:, None, :, None]).reshape(
        group_tok, 2, used_n * rank_n
    )
    gate_adapter_rows = jnp.dot(
        spread[:, 0],
        fetch_gb.reshape(used_n * rank_n, hidden_local),
        preferred_element_type=jnp.float32,
    )
    up_adapter_rows = jnp.dot(
        spread[:, 1],
        fetch_ub.reshape(used_n * rank_n, hidden_local),
        preferred_element_type=jnp.float32,
    )
    gate_preactivation = plain_output[:, :hidden_local] + adapter_scale * gate_adapter_rows
    up_preactivation = plain_output[:, hidden_local:] + adapter_scale * up_adapter_rows
    hidden = (jax.nn.silu(gate_preactivation) * up_preactivation).astype(jnp.bfloat16)
    down_total_sum = lax.psum_scatter(
        jnp.dot(hidden, w_down, preferred_element_type=jnp.float32).astype(jnp.bfloat16),
        "tensor",
        scatter_dimension=0,
        tiled=True,
    ).astype(jnp.float32)
    down_adapter_rows = jnp.dot(
        hidden, to_columns(fetch_da), preferred_element_type=jnp.float32
    ).reshape(group_tok, used_n, rank_n)
    partial_down = jnp.sum(down_adapter_rows * token_weights[:, :, None], axis=1)
    mid_down = lax.psum_scatter(
        partial_down.astype(jnp.bfloat16), "tensor", scatter_dimension=0, tiled=True
    )
    spread_down = (mid_down[:, None, :] * own_weights.astype(jnp.bfloat16)[:, :, None]).reshape(
        tok_dev, used_n * rank_n
    )
    adapter_down_term = jnp.dot(
        spread_down,
        fetch_db.reshape(used_n * rank_n, fetch_db.shape[2]),
        preferred_element_type=jnp.float32,
    )
    return (residual_float + down_total_sum + adapter_scale * adapter_down_term).astype(
        jnp.bfloat16
    )[None]


def solution(mesh):
    placed = (
        P("seq", "tensor", None),
        P(),
        P(None, "tensor"),
        P(None, "tensor"),
        P("tensor", None),
        P("seq", "tensor", None),
        P("seq", None, "tensor"),
        P("seq", "tensor", None),
        P("seq", None, "tensor"),
        P("seq", "tensor", None),
        P("seq", None, None),
        P("seq", None),
        P("seq", None),
        P(),
        P(),
    )
    return jax.shard_map(
        local, mesh=mesh, in_specs=placed, out_specs=P("seq", "tensor", None), check_vma=False
    )
```

profile of v0, /device:TPU:0, one launch (start us, length us, event | category | flops | bytes accessed | tf_op | source)
XLA Modules:
  0.0 239.0 jit_solution(9655191861748860964)
XLA Ops:
  9.0 20.8 %all_gather.26 = bf16[16,1368,16]{1,2,0:T(8,128)(2,1)S(1)} all-gather(bf16[4,1368,16]{1,2,0:T(8,128)(2,1)} %param.24), channel_id=1, replica_groups=mesh['tensor'=8,'seq'=4] {'seq'}, dimensions={0}, use_global_device_ids=true | all-gather | bytes 875520 | tf_op jit(solution)/shard_map/all_gather | solution.py:52
  29.8 4.4 %copy.58 = bf16[16,1368,16]{2,1,0:T(8,128)(2,1)} copy(bf16[16,1368,16]{1,2,0:T(8,128)(2,1)S(1)} %all_gather.26) | data formatting | bytes 1400832 | tf_op jit(solution)/shard_map/all_gather | solution.py:52
  34.2 5.5 %reshape.168 = bf16[16,21888]{1,0:T(8,128)(2,1)S(1)} reshape(bf16[16,1368,16]{2,1,0:T(8,128)(2,1)} %copy.58) | data formatting | bytes 1400832 | tf_op jit(solution)/shard_map/reshape | solution.py:10
  40.4 5.7 %reshape.169 = bf16[16,1368,16]{2,1,0:T(8,128)(2,1)} reshape(bf16[16,21888]{1,0:T(8,128)(2,1)S(1)} %convolution_convert_fusion.1) | data formatting | bytes 1400832 | tf_op jit(solution)/shard_map/reshape | solution.py:12
  46.1 6.0 %copy.59 = bf16[1368,16,16]{0,2,1:T(8,128)(2,1)} copy(bf16[1368,16,16]{2,0,1:T(8,128)(2,1)} %bitcast.56) | data formatting | bytes 1400832 | tf_op jit(solution)/shard_map/transpose | solution.py:17
  52.3 9.9 %all_gather.21 = bf16[128,2048]{1,0:T(8,128)(2,1)S(1)} all-gather(bf16[16,2048]{1,0:T(8,128)(2,1)S(1)} %fusion.16), channel_id=1, replica_groups=mesh['tensor'=8,'seq'=4] {'tensor'}, dimensions={0}, use_global_device_ids=true | all-gather | bytes 589824 | tf_op jit(solution)/shard_map/all_gather | solution.py:76
  62.2 17.6 %all_gather.25 = bf16[16,16,1368]{2,1,0:T(8,128)(2,1)S(1)} all-gather(bf16[4,16,1368]{2,1,0:T(8,128)(2,1)S(1)} %copy-done.2), channel_id=1, replica_groups=mesh['tensor'=8,'seq'=4] {'seq'}, dimensions={0}, use_global_device_ids=true | all-gather | bytes 875520 | tf_op jit(solution)/shard_map/all_gather | solution.py:51
  80.9 2.1 reshape_reshape.10
  83.0 5.1 %fusion.29 = f32[128,1368]{0,1:T(8,128)} fusion(bf16[128,2048]{1,0:T(8,128)(2,1)S(1)} %all_gather.21, bf16[2048,1368]{0,1:T(8,128)(2,1)} %param.18), kind=kOutput, calls=%fused_computation.58 | convolution fusion | flops 717225984 | bytes 6828032 | tf_op jit(solution)/shard_map/dot_general | solution.py:78
  88.1 4.2 %fusion.28 = f32[128,1368]{0,1:T(8,128)S(1)} fusion(bf16[128,2048]{1,0:T(8,128)(2,1)S(1)} %all_gather.21, bf16[2048,1368]{0,1:T(8,128)(2,1)} %param.17), kind=kOutput, calls=%fused_computation.57 | convolution fusion | flops 717225984 | bytes 6828032 | tf_op jit(solution)/shard_map/dot_general | solution.py:77
  92.3 17.6 %all_gather.24 = bf16[16,16,1368]{2,1,0:T(8,128)(2,1)S(1)} all-gather(bf16[4,16,1368]{2,1,0:T(8,128)(2,1)S(1)} %copy-done.3), channel_id=1, replica_groups=mesh['tensor'=8,'seq'=4] {'seq'}, dimensions={0}, use_global_device_ids=true | all-gather | bytes 875520 | tf_op jit(solution)/shard_map/all_gather | solution.py:50
  111.0 1.2 reshape_reshape.9
  112.2 13.6 %all_gather.23 = bf16[16,256,16]{1,2,0:T(8,128)(2,1)S(1)} all-gather(bf16[4,256,16]{1,2,0:T(8,128)(2,1)S(1)} %copy-done.4), channel_id=1, replica_groups=mesh['tensor'=8,'seq'=4] {'seq'}, dimensions={0}, use_global_device_ids=true | all-gather | bytes 163840 | tf_op jit(solution)/shard_map/all_gather | solution.py:49
  126.3 1.8 reshape.160
  129.5 13.3 %all_gather.22 = bf16[16,256,16]{1,2,0:T(8,128)(2,1)S(1)} all-gather(bf16[4,256,16]{1,2,0:T(8,128)(2,1)S(1)} %copy-done.5), channel_id=1, replica_groups=mesh['tensor'=8,'seq'=4] {'seq'}, dimensions={0}, use_global_device_ids=true | all-gather | bytes 163840 | tf_op jit(solution)/shard_map/all_gather | solution.py:48
  143.3 1.8 reshape.157
  145.3 0.8 reshape.158
  146.8 12.1 %psum.7 = bf16[128,2,16]{0,2,1:T(8,128)(2,1)S(1)} all-reduce(bf16[128,2,16]{0,2,1:T(8,128)(2,1)S(1)} %multiply_reduce_fusion), channel_id=1, replica_groups=mesh['tensor'=8,'seq'=4] {'tensor'}, use_global_device_ids=true, to_apply=%region_6.7 | all-reduce | flops 4096 | bytes 16384 | tf_op jit(solution)/shard_map/psum | solution.py:85
  159.4 1.8 fusion.3
  163.1 4.5 %convolution_convert_fusion.6 = bf16[128,2048]{1,0:T(8,128)(2,1)} fusion(bf16[128,1368]{0,1:T(8,128)(2,1)S(1)} %fusion.3, bf16[1368,2048]{1,0:T(8,128)(2,1)} %param.19), kind=kOutput, calls=%fused_computation.12 | convolution fusion | flops 717488128 | bytes 6477824 | tf_op jit(solution)/shard_map/dot_general | solution.py:104
  167.8 24.5 %reduce-scatter.7.cloned.1.call-done = bf16[16,16]{1,0:T(8,128)(2,1)} async-done(((bf16[128,16]{1,0:T(8,128)(2,1)}), bf16[16,16]{1,0:T(8,128)(2,1)}) %reduce-scatter.7.cloned.1.call-update) | async-done | bytes 528 | tf_op jit(solution)/shard_map/reduce_scatter | solution.py:113
  193.2 1.8 copy.65
  196.1 33.8 %reduce-scatter.5.cloned.1.call-done = bf16[16,2048]{1,0:T(8,128)(2,1)} async-done(((bf16[128,2048]{1,0:T(8,128)(2,1)}), bf16[16,2048]{1,0:T(8,128)(2,1)}) %reduce-scatter.5.cloned.1.call-update) | async-done | bytes 65552 | tf_op jit(solution)/shard_map/reduce_scatter | solution.py:103
  229.9 1.7 fusion.6
  (59 shorter events, 12.2 us)
Async XLA Ops:
  7.4 184.9 %reduce-scatter.7.cloned.1.call-start = ((), (), s32[]{:S(2)}) async-start(), calls=%async_computation.4 | async-start | bytes 36864 | tf_op jit(solution)/shard_map/reduce_scatter | solution.py:113
  29.8 9.9 %copy-start.7 = (s32[16]{0:T(128)S(1)}, s32[16]{0:T(128)}, u32[]{:S(2)}) copy-start(s32[16]{0:T(128)} %param.29) | copy-start | bytes 196
  29.8 9.9 %copy-start.8 = (s32[16]{0:T(128)S(1)}, s32[16]{0:T(128)}, u32[]{:S(2)}) copy-start(s32[16]{0:T(128)} %param.28) | copy-start | bytes 196
  40.3 11.7 %copy-start.6 = (bf16[2048]{0:T(1024)(128)(2,1)S(1)}, bf16[2048]{0:T(1024)(128)(2,1)}, u32[]{:S(2)}) copy-start(bf16[2048]{0:T(1024)(128)(2,1)} %param.16) | copy-start | bytes 12292
  40.3 11.7 %copy-start.1 = (bf16[1,16,2048]{2,1,0:T(8,128)(2,1)S(1)}, bf16[1,16,2048]{2,1,0:T(8,128)(2,1)}, u32[]{:S(2)}) copy-start(bf16[1,16,2048]{2,1,0:T(8,128)(2,1)} %param.15) | copy-start | bytes 196612
  40.3 21.8 %copy-start.2 = (bf16[4,16,1368]{2,1,0:T(8,128)(2,1)S(1)}, bf16[4,16,1368]{2,1,0:T(8,128)(2,1)}, u32[]{:S(2)}) copy-start(bf16[4,16,1368]{2,1,0:T(8,128)(2,1)} %param.23) | copy-start | bytes 525316
  82.9 9.4 %copy-start.3 = (bf16[4,16,1368]{2,1,0:T(8,128)(2,1)S(1)}, bf16[4,16,1368]{2,1,0:T(8,128)(2,1)}, u32[]{:S(2)}) copy-start(bf16[4,16,1368]{2,1,0:T(8,128)(2,1)} %param.21) | copy-start | bytes 525316
  88.1 24.1 %copy-start.4 = (bf16[4,256,16]{1,2,0:T(8,128)(2,1)S(1)}, bf16[4,256,16]{1,2,0:T(8,128)(2,1)}, u32[]{:S(2)}) copy-start(bf16[4,256,16]{1,2,0:T(8,128)(2,1)} %param.22) | copy-start | bytes 98308
  92.3 37.2 %copy-start.5 = (bf16[4,256,16]{1,2,0:T(8,128)(2,1)S(1)}, bf16[4,256,16]{1,2,0:T(8,128)(2,1)}, u32[]{:S(2)}) copy-start(bf16[4,256,16]{1,2,0:T(8,128)(2,1)} %param.20) | copy-start | bytes 98308
  146.5 14.6 %copy-start = (bf16[1368,16,16]{0,2,1:T(8,128)(2,1)S(1)}, bf16[1368,16,16]{0,2,1:T(8,128)(2,1)}, u32[]{:S(2)}) copy-start(bf16[1368,16,16]{0,2,1:T(8,128)(2,1)} %copy.59) | copy-start | bytes 2101252
  162.3 31.0 %all-gather.2.cloned.1.call-start = ((), (), s32[]{:S(2)}) async-start(), calls=%async_computation.3 | async-start | bytes 1310720 | tf_op jit(solution)/shard_map/all_gather | solution.py:53
  162.8 67.0 %reduce-scatter.5.cloned.1.call-start = ((), (), s32[]{:S(2)}) async-start(), calls=%async_computation.2 | async-start | bytes 589824 | tf_op jit(solution)/shard_map/reduce_scatter | solution.py:103
Sparse Core Ops, SparseCore 0:
  162.4 29.8 reduce-scatter.6
  195.7 34.1 reduce-scatter.4
Sparse Core Ops, SparseCore 1:
  164.4 26.5 all-gather.1
where the time goes:
time: 240 us; the launch traced here: 239 us
  blocking collectives  105 us (44%)
  waiting for transfers between devices  58.8 us (24%)
  local copies, waits for them, and re-layouts  36.4 us (15%)
  matrix products  20.5 us (9%)
  between operations  15.1 us (6%)
  other arithmetic  2.89 us (1%)
    reduce_scatter x1, waiting for transfers between devices, local(): lax.psum_scatter(jnp.dot(hidden, w_down, preferred_element_type=jnp.float...  33.8 us
    reduce_scatter x1, waiting for transfers between devices, local(): lax.psum_scatter(partial_down.astype(jnp.bfloat16), 'tensor', scatter_dim...  24.5 us
    all_gather x1, blocking collectives, local(): lax.all_gather(down_a, 'seq', axis=0, tiled=True)  20.8 us
    all_gather x1, blocking collectives, local(): lax.all_gather(up_b, 'seq', axis=0, tiled=True)  17.6 us
    all_gather x1, blocking collectives, local(): lax.all_gather(gate_b, 'seq', axis=0, tiled=True)  17.6 us
    all_gather x1, blocking collectives, local(): lax.all_gather(up_a, 'seq', axis=0, tiled=True)  13.6 us
    all_gather x1, blocking collectives, local(): lax.all_gather(gate_a, 'seq', axis=0, tiled=True)  13.3 us
    psum x1, blocking collectives, local(): mids = lax.psum(partial_mid.astype(jnp.bfloat16), 'tensor')  12.1 us
  transfers between devices with their start and end apart: 3, of which 2 were waited for; matrix products, arithmetic and copies ran while one was open for 4% of the time, Pallas kernels for 0%

commit v1 on v0

v1 whole, which is shorter than its diff:
```python
import functools

import jax
import jax.numpy as jnp
from jax import lax
from jax.experimental import pallas as pl
from jax.experimental.pallas import tpu as pltpu
from jax.sharding import PartitionSpec as P

adapter_scale = 0.5
MESH = pl.DeviceIdType.MESH
COL_TILE = 256
SUM_CHUNKS = 4
NT = (((1,), (1,)), ((), ()))
NN = (((1,), (0,)), ((), ()))


def mm(a, b, dims):
    return lax.dot_general(a, b, dims, preferred_element_type=jnp.float32)


def tiles(width, body):
    full = width // COL_TILE

    def step(i, carry):
        body(pl.ds(pl.multiple_of(i * COL_TILE, COL_TILE), COL_TILE))
        return carry

    if full:
        lax.fori_loop(0, full, step, 0)
    if width % COL_TILE:
        body(pl.ds(full * COL_TILE, width % COL_TILE))


def kernel(
    tensor_n,
    pair_n,
    resid_ref,
    gain_ref,
    wg_hbm,
    wu_hbm,
    wd_hbm,
    ga_ref,
    gb_ref,
    ua_ref,
    ub_ref,
    da_ref,
    db_ref,
    lengths_ref,
    choice_ref,
    used_ref,
    holder_ref,
    out_ref,
    wg,
    wu,
    wd,
    x,
    ga,
    gb,
    ua,
    ub,
    da,
    db,
    slots_own,
    slots_far,
    mid_own,
    mid_in,
    pre_g,
    pre_u,
    hidden,
    y,
    y_in,
    z_out,
    z_in,
    kept,
    w_sem,
    own_sem,
    x_send,
    x_recv,
    far_send,
    far_recv,
    ad_send,
    ad_recv,
    mid_send,
    mid_recv,
    y_send,
    y_recv,
):
    k = lax.axis_index("tensor")
    s = lax.axis_index("seq")
    half = s // pair_n
    place = lax.rem(s, pair_n)
    far = {"seq": (1 - half) * pair_n + place}
    tok_dev, width = resid_ref.shape
    group_tok = tok_dev * tensor_n
    toks = 2 * group_tok
    stored_rows, hidden_local = gb_ref.shape
    rank_n = mid_own.shape[0] // 2
    rows = pair_n * stored_rows
    slots_n = rows // rank_n
    feat_loc = ga_ref.shape[1]
    chunk = width // SUM_CHUNKS

    def peer(d):
        return {"tensor": lax.rem(k + d, tensor_n)}

    def mate(d):
        return {"seq": half * pair_n + lax.rem(place + d, pair_n)}

    weights = [
        pltpu.make_async_copy(wg_hbm, wg, w_sem.at[0]),
        pltpu.make_async_copy(wu_hbm, wu, w_sem.at[1]),
        pltpu.make_async_copy(wd_hbm, wd, w_sem.at[2]),
    ]
    for copy in weights:
        copy.start()
    pairs = [(ga_ref, ga), (ua_ref, ua), (gb_ref, gb), (ub_ref, ub), (da_ref, da), (db_ref, db)]
    own_copies = [
        pltpu.make_async_copy(src, dst.at[place], own_sem.at[i])
        for i, (src, dst) in enumerate(pairs)
    ]
    for copy in own_copies:
        copy.start()

    barrier = pltpu.get_barrier_semaphore()
    for d in range(1, tensor_n):
        pl.semaphore_signal(barrier, inc=1, device_id=peer(d), device_id_type=MESH)
    for d in range(1, pair_n):
        pl.semaphore_signal(barrier, inc=1, device_id=mate(d), device_id_type=MESH)
    pl.semaphore_signal(barrier, inc=1, device_id=far, device_id_type=MESH)

    res = resid_ref[...].astype(jnp.float32)
    scale = lax.rsqrt(jnp.mean(res * res, axis=-1, keepdims=True) + 1e-06)
    x[0, k] = (res * scale * gain_ref[...].astype(jnp.float32)).astype(jnp.bfloat16)

    position = lax.broadcasted_iota(jnp.int32, (8, group_tok), 1)
    slot_line = jnp.zeros((8, group_tok), jnp.float32)
    end = jnp.int32(0)
    for p in range(lengths_ref.shape[1]):
        slot = holder_ref[used_ref[choice_ref[0, p]]]
        first, end = end, end + lengths_ref[0, p]
        inside = jnp.logical_and(position >= first, position < end)
        slot_line = jnp.where(inside, slot.astype(jnp.float32), slot_line)
    slots_own[...] = slot_line

    pl.semaphore_wait(barrier, tensor_n - 1 + pair_n - 1 + 1)

    sends = []

    def remote(src, dst, send_sem, recv_sem, device):
        copy = pltpu.make_async_remote_copy(
            src_ref=src,
            dst_ref=dst,
            send_sem=send_sem,
            recv_sem=recv_sem,
            device_id=device,
            device_id_type=MESH,
        )
        return copy

    def send(*args):
        copy = remote(*args)
        copy.start()
        sends.append(copy)

    send(x.at[0, k], x.at[1, k], far_send.at[0], far_recv.at[0], far)
    for d in range(1, tensor_n):
        send(x.at[0, k], x.at[0, k], x_send.at[0, d - 1], x_recv.at[0, d - 1], peer(d))
    send(slots_own, slots_far, far_send.at[1], far_recv.at[1], far)
    for i, (src, dst) in enumerate(pairs):
        for d in range(1, pair_n):
            send(src, dst.at[place], ad_send.at[i, d - 1], ad_recv.at[i, d - 1], mate(d))

    def wait_pair(i):
        own_copies[i].wait()
        src, dst = pairs[i]
        for d in range(1, pair_n):
            origin = lax.rem(place - d + pair_n, pair_n)
            remote(
                src, dst.at[origin], ad_send.at[i, d - 1], ad_recv.at[i, d - 1], mate(d)
            ).wait_recv()

    remote(x.at[0, k], x.at[1, k], far_send.at[0], far_recv.at[0], far).wait_recv()
    for d in range(1, tensor_n):
        send(x.at[1, k], x.at[1, k], x_send.at[1, d - 1], x_recv.at[1, d - 1], peer(d))
    for h in range(2):
        for d in range(1, tensor_n):
            origin = lax.rem(k - d + tensor_n, tensor_n)
            remote(
                x.at[h, k], x.at[h, origin], x_send.at[h, d - 1], x_recv.at[h, d - 1], peer(d)
            ).wait_recv()
    remote(slots_own, slots_far, far_send.at[1], far_recv.at[1], far).wait_recv()

    base = (half * (pair_n * (stored_rows // rank_n))).astype(jnp.float32)
    line = jnp.concatenate([slots_own[...], slots_far[...]], axis=1) - base
    line_rows = jnp.broadcast_to(line[0:1, :], (rows, toks))
    row_slot = (lax.broadcasted_iota(jnp.int32, (rows, toks), 0) // rank_n).astype(jnp.float32)
    mask_t = line_rows == row_slot

    wait_pair(0)
    wait_pair(1)
    copies = max(1, 128 // feat_loc)
    span = copies * feat_loc
    mine = x[:, :, :, pl.ds(pl.multiple_of(k // copies * span, span), span)].reshape(toks, span)
    for i, a_ref in enumerate((ga, ua)):
        a = a_ref[...].reshape(rows, feat_loc)
        if copies > 1:
            a = jnp.concatenate([a] * copies, axis=1)
            part = lax.broadcasted_iota(jnp.int32, (rows, span), 1) // feat_loc
            a = jnp.where(part == lax.rem(k, copies), a, jnp.zeros_like(a))
        low = mm(a, mine, NT)
        low = jnp.where(mask_t, low, 0.0).reshape(slots_n, rank_n, toks)
        mid_own[pl.ds(i * rank_n, rank_n), :] = jnp.sum(low, axis=0).astype(jnp.bfloat16)
    for d in range(1, tensor_n):
        send(mid_own, mid_in.at[d - 1], mid_send.at[d - 1], mid_recv.at[d - 1], peer(d))

    weights[0].wait()
    weights[1].wait()

    def project(cols):
        block = x[...].reshape(toks, width)
        pre_g[:, cols] = mm(block, wg[cols, :], NT)
        pre_u[:, cols] = mm(block, wu[cols, :], NT)

    tiles(hidden_local, project)

    mid = mid_own[...].astype(jnp.float32)
    for d in range(1, tensor_n):
        remote(
            mid_own, mid_in.at[d - 1], mid_send.at[d - 1], mid_recv.at[d - 1], peer(d)
        ).wait_recv()
        mid = mid + mid_in[d - 1].astype(jnp.float32)
    mid = mid.astype(jnp.bfloat16).astype(jnp.float32)
    spreads = []
    for i in range(2):
        part = mid[i * rank_n : (i + 1) * rank_n][None]
        part = jnp.broadcast_to(part, (slots_n, rank_n, toks)).reshape(rows, toks)
        part = jnp.where(mask_t, adapter_scale * part, 0.0)
        spreads.append(part.T.astype(jnp.bfloat16))
    slot_cols = line_rows[: min(rows, 128)].T[:, 0:1]
    held = jnp.logical_and(slot_cols >= 0.0, slot_cols < float(slots_n))
    wait_pair(2)
    wait_pair(3)

    def activate(cols):
        wide = cols.size
        g = pre_g[:, cols] + mm(spreads[0], gb[:, :, cols].reshape(rows, wide), NN)
        u = pre_u[:, cols] + mm(spreads[1], ub[:, :, cols].reshape(rows, wide), NN)
        h = g / (1.0 + jnp.exp(-g)) * u
        hidden[:, cols] = jnp.where(held, h, 0.0).astype(jnp.bfloat16)

    tiles(hidden_local, activate)

    wait_pair(4)
    low = mm(hidden[...], da[...].reshape(rows, hidden_local), NT)
    col_slot = (lax.broadcasted_iota(jnp.int32, (toks, rows), 1) // rank_n).astype(jnp.float32)
    low = jnp.where(slot_cols == col_slot, adapter_scale * low, 0.0).astype(jnp.bfloat16)
    wait_pair(5)
    weights[2].wait()
    for c in range(SUM_CHUNKS):
        cols = pl.ds(c * chunk, chunk)
        part = mm(hidden[...], wd[:, cols], NN) + mm(low, db[:, :, cols].reshape(rows, chunk), NN)
        y[:, :, :, cols] = part.astype(jnp.bfloat16).reshape(2, tensor_n, tok_dev, chunk)
        for d in range(1, tensor_n):
            to = lax.rem(k + d, tensor_n)
            send(
                y.at[:, to, :, cols],
                y_in.at[d - 1, :, :, cols],
                y_send.at[c, d - 1],
                y_recv.at[c, d - 1],
                peer(d),
            )
    for c in range(SUM_CHUNKS):
        cols = pl.ds(c * chunk, chunk)
        total = y[:, k, :, cols].astype(jnp.float32)
        for d in range(1, tensor_n):
            remote(
                y.at[:, k, :, cols],
                y_in.at[d - 1, :, :, cols],
                y_send.at[c, d - 1],
                y_recv.at[c, d - 1],
                peer(d),
            ).wait_recv()
            total = total + y_in[d - 1, :, :, cols].astype(jnp.float32)
        z_out[c] = total[1].astype(jnp.bfloat16)
        send(z_out.at[c], z_in.at[c], far_send.at[2 + c], far_recv.at[2 + c], far)
        kept[:, cols] = total[0]
    for c in range(SUM_CHUNKS):
        cols = pl.ds(c * chunk, chunk)
        remote(z_out.at[c], z_in.at[c], far_send.at[2 + c], far_recv.at[2 + c], far).wait_recv()
        whole = resid_ref[:, cols].astype(jnp.float32) + kept[:, cols] + z_in[c].astype(jnp.float32)
        out_ref[:, cols] = whole.astype(jnp.bfloat16)
    for copy in sends:
        copy.wait_send()


def local(
    pair_n,
    resid,
    norm_gain,
    gate_weight_matrix,
    up_weight,
    w_down,
    gate_a,
    gate_b,
    up_a,
    up_b,
    down_a,
    down_b,
    prompt_lengths,
    prompt_choice,
    used_adapters,
    adapter_holder,
):
    tensor_n = lax.axis_size("tensor")
    _, tok_dev, width = resid.shape
    stored, feat_loc, rank_n = gate_a.shape
    hidden_local = gate_weight_matrix.shape[1]
    toks = 2 * tok_dev * tensor_n
    rows = stored * rank_n
    bf = jnp.bfloat16

    def by_row(a):
        return jnp.transpose(a, (0, 2, 1)).reshape(rows, a.shape[1])

    def flat(b):
        return b.reshape(rows, b.shape[2])

    vmem = pl.BlockSpec(memory_space=pltpu.VMEM)
    smem = pl.BlockSpec(memory_space=pltpu.SMEM)
    hbm = pl.BlockSpec(memory_space=pl.ANY)
    dma = pltpu.SemaphoreType.DMA
    chunk = width // SUM_CHUNKS
    out = pl.pallas_call(
        functools.partial(kernel, tensor_n, pair_n),
        out_shape=jax.ShapeDtypeStruct((tok_dev, width), bf),
        in_specs=[vmem, vmem, hbm, hbm, hbm] + [vmem] * 6 + [smem] * 4,
        out_specs=vmem,
        scratch_shapes=[
            pltpu.VMEM((hidden_local, width), bf),
            pltpu.VMEM((hidden_local, width), bf),
            pltpu.VMEM((hidden_local, width), bf),
            pltpu.VMEM((2, tensor_n, tok_dev, width), bf),
            pltpu.VMEM((pair_n, rows, feat_loc), bf),
            pltpu.VMEM((pair_n, rows, hidden_local), bf),
            pltpu.VMEM((pair_n, rows, feat_loc), bf),
            pltpu.VMEM((pair_n, rows, hidden_local), bf),
            pltpu.VMEM((pair_n, rows, hidden_local), bf),
            pltpu.VMEM((pair_n, rows, width), bf),
            pltpu.VMEM((8, toks // 2), jnp.float32),
            pltpu.VMEM((8, toks // 2), jnp.float32),
            pltpu.VMEM((2 * rank_n, toks), bf),
            pltpu.VMEM((tensor_n - 1, 2 * rank_n, toks), bf),
            pltpu.VMEM((toks, hidden_local), jnp.float32),
            pltpu.VMEM((toks, hidden_local), jnp.float32),
            pltpu.VMEM((toks, hidden_local), bf),
            pltpu.VMEM((2, tensor_n, tok_dev, width), bf),
            pltpu.VMEM((tensor_n - 1, 2, tok_dev, width), bf),
            pltpu.VMEM((SUM_CHUNKS, tok_dev, chunk), bf),
            pltpu.VMEM((SUM_CHUNKS, tok_dev, chunk), bf),
            pltpu.VMEM((tok_dev, width), jnp.float32),
            dma((3,)),
            dma((6,)),
            dma((2, tensor_n - 1)),
            dma((2, tensor_n - 1)),
            dma((2 + SUM_CHUNKS,)),
            dma((2 + SUM_CHUNKS,)),
            dma((6, max(1, pair_n - 1))),
            dma((6, max(1, pair_n - 1))),
            dma((tensor_n - 1,)),
            dma((tensor_n - 1,)),
            dma((SUM_CHUNKS, tensor_n - 1)),
            dma((SUM_CHUNKS, tensor_n - 1)),
        ],
        compiler_params=pltpu.CompilerParams(
            collective_id=0, has_side_effects=True, vmem_limit_bytes=60 * 2**20
        ),
        name="ffn",
    )(
        resid[0],
        norm_gain[None],
        gate_weight_matrix.T,
        up_weight.T,
        w_down,
        by_row(gate_a),
        flat(gate_b),
        by_row(up_a),
        flat(up_b),
        by_row(down_a),
        flat(down_b),
        prompt_lengths,
        prompt_choice,
        used_adapters,
        adapter_holder,
    )
    return out[None]


def solution(mesh):
    placed = (
        P("seq", "tensor", None),
        P(),
        P(None, "tensor"),
        P(None, "tensor"),
        P("tensor", None),
        P("seq", "tensor", None),
        P("seq", None, "tensor"),
        P("seq", "tensor", None),
        P("seq", None, "tensor"),
        P("seq", "tensor", None),
        P("seq", None, None),
        P("seq", None),
        P("seq", None),
        P(),
        P(),
    )
    return jax.shard_map(
        functools.partial(local, mesh.shape["seq"] // 2),
        mesh=mesh,
        in_specs=placed,
        out_specs=P("seq", "tensor", None),
        check_vma=False,
    )
```

time: 240 us -> 51.1 us (0.21)
  blocking collectives: 105 us -> 0 us
  waiting for transfers between devices: 58.8 us -> 0 us
  Pallas kernels: 0 us -> 48.1 us
  local copies, waits for them, and re-layouts: 36.4 us -> 2.76 us
  matrix products: 20.5 us -> 0 us
  between operations: 15.1 us -> 0.01 us
  other arithmetic: 2.89 us -> 0 us
    all_gather x6 -> x0, blocking collectives: 92.9 us -> none  [the longest x1 20.8 us: local(): lax.all_gather(down_a, 'seq', axis=0, tiled=True)]
    reduce_scatter x2 -> x0, waiting for transfers between devices: 58.3 us -> none  [the longest x1 33.8 us: local(): lax.psum_scatter(jnp.dot(hidden, w_down, preferred_element_type=jnp.float...]
    pallas_call x0 -> x1, Pallas kernels: none -> 48.1 us  [local(): pl.pallas_call(functools.partial(kernel, tensor_n, pair_n), out_shape=jax...]
    dot_general x14 -> x0, matrix products: 20.5 us -> none  [the longest x1 5.12 us: local(): up_part = jnp.dot(piece, up_weight, preferred_element_type=jnp.float32)]
    reshape x8 -> x0, local copies, waits for them, and re-layouts: 17.7 us -> none  [the longest x5 10.4 us: choose(): flat = stacked.reshape(stacked.shape[0], -1)]
    psum x1 -> x0, blocking collectives: 12.1 us -> none  [local(): mids = lax.psum(partial_mid.astype(jnp.bfloat16), 'tensor')]
    transpose x3 -> x0, local copies, waits for them, and re-layouts: 6.62 us -> none  [to_columns(): return jnp.transpose(stacked, (1, 0, 2)).reshape(inner, used_n * rank_n)]
    all_gather x3 -> x0, local copies, waits for them, and re-layouts: 5.35 us -> none  [the longest x1 4.4 us: local(): lax.all_gather(down_a, 'seq', axis=0, tiled=True)]
  transfers between devices with their start and end apart: 3 -> 0, of which waited for: 2 -> 0; matrix products, arithmetic and copies ran while one was open for 4% -> 0% of each run, Pallas kernels for 0% -> 0%
where the time goes in v1:
time: 51.1 us; the launch traced here: 50.9 us
  Pallas kernels  48.1 us (94%)
  local copies, waits for them, and re-layouts  2.76 us (5%)
    pallas_call x1, Pallas kernels, local(): pl.pallas_call(functools.partial(kernel, tensor_n, pair_n), out_shape=jax...  48.1 us
    unnamed x1, local copies, waits for them, and re-layouts  1.47 us
    broadcast_in_dim x1, local copies, waits for them, and re-layouts, local(): norm_gain[None]  1.29 us

profile of v1, /device:TPU:0, one launch (start us, length us, event | category | flops | bytes accessed | tf_op | source)
XLA Modules:
  0.0 50.9 jit_solution(14101039994414565288)
XLA Ops:
  0.0 1.3 %broadcast_in_dim.6.gain_ref = bf16[1,2048]{1,0:T(2,128)(2,1)} reshape(bf16[2048]{0:T(1024)(128)(2,1)} %param.16) | data formatting | bytes 8192 | tf_op jit(solution)/shard_map/broadcast_in_dim | solution.py:381
  1.3 48.1 %ffn.1 = bf16[16,2048]{1,0:T(8,128)(2,1)} custom-call(bf16[16,2048]{1,0:T(8,128)(2,1)} %bitcast.23, bf16[1,2048]{1,0:T(2,128)(2,1)} %broadcast_in_dim.6.gain_ref, bf16[1368,2048]{1,0:T(8,128)(2,1)} %bitcast.16, bf16[1368,2048]{1,0:T(8,128)(2,1)} %bitcast.17, bf16[1368,2048]{1,0:T(8,128)(2,1)} %wd_hbm.1, bf16[64,256]{1,0:T(8,128)(2,1)} %bitcast.24, ...), custom_call_target="tpu_custom_call" | custom-call | tf_op jit(solution)/shard_map/ffn/pallas_call | solution.py:334
  49.4 1.5 %copy.17 = bf16[1,16,2048]{2,1,0:T(8,128)(2,1)} copy(bf16[1,16,2048]{2,1,0:T(8,128)(2,1)} %bitcast.19) | data formatting | bytes 131072

commit v2 on v1

--- a/solution.py
+++ b/solution.py
@@ -69,6 +69,8 @@
     pre_u,
     hidden,
     y,
+    y_pair,
+    y_sum,
     y_in,
     z_out,
     z_in,
@@ -85,6 +87,8 @@
     mid_recv,
     y_send,
     y_recv,
+    pair_send,
+    pair_recv,
 ):
     k = lax.axis_index("tensor")
     s = lax.axis_index("seq")
@@ -101,8 +105,21 @@
     feat_loc = ga_ref.shape[1]
     chunk = width // SUM_CHUNKS
 
+    chips = tensor_n // 2
+    chip, core = k // 2, lax.rem(k, 2)
+    sibling = {"tensor": chip * 2 + 1 - core}
+
     def peer(d):
         return {"tensor": lax.rem(k + d, tensor_n)}
+
+    def chip_after(d):
+        return lax.rem(chip + d, chips)
+
+    def chip_before(d):
+        return lax.rem(chip - d + chips, chips)
+
+    def across(d):
+        return {"tensor": chip_after(d) * 2 + core}
 
     def mate(d):
         return {"seq": half * pair_n + lax.rem(place + d, pair_n)}
@@ -164,12 +181,45 @@
         sends.append(copy)
 
     send(x.at[0, k], x.at[1, k], far_send.at[0], far_recv.at[0], far)
-    for d in range(1, tensor_n):
-        send(x.at[0, k], x.at[0, k], x_send.at[0, d - 1], x_recv.at[0, d - 1], peer(d))
+
+    def block(h, index, j, device):
+        return x.at[h, index], x.at[h, index], x_send.at[h, j], x_recv.at[h, j], device
+
+    def spread_block(h):
+        for d in range(1, chips):
+            send(*block(h, k, d, across(d)))
+        send(*block(h, k, 0, sibling))
+
+    spread_block(0)
     send(slots_own, slots_far, far_send.at[1], far_recv.at[1], far)
-    for i, (src, dst) in enumerate(pairs):
+    share = width // 2
+    own_share = pl.ds(pl.multiple_of(core * share, share), share)
+    other_share = pl.ds(pl.multiple_of((1 - core) * share, share), share)
+    last = len(pairs) - 1
+    for i, (src, dst) in enumerate(pairs[:last]):
         for d in range(1, pair_n):
             send(src, dst.at[place], ad_send.at[i, d - 1], ad_recv.at[i, d - 1], mate(d))
+
+    def half_of(origin, d, cols):
+        return (
+            db_ref.at[:, cols],
+            db.at[origin, :, cols],
+            ad_send.at[last, d - 1],
+            ad_recv.at[last, d - 1],
+            mate(d),
+        )
+
+    def handed(origin, d, cols):
+        return (
+            db.at[origin, :, cols],
+            db.at[origin, :, cols],
+            ad_send.at[last + 1, d - 1],
+            ad_recv.at[last + 1, d - 1],
+            sibling,
+        )
+
+    for d in range(1, pair_n):
+        send(*half_of(place, d, own_share))
 
     def wait_pair(i):
         own_copies[i].wait()
@@ -181,14 +231,17 @@
             ).wait_recv()
 
     remote(x.at[0, k], x.at[1, k], far_send.at[0], far_recv.at[0], far).wait_recv()
-    for d in range(1, tensor_n):
-        send(x.at[1, k], x.at[1, k], x_send.at[1, d - 1], x_recv.at[1, d - 1], peer(d))
+    spread_block(1)
     for h in range(2):
-        for d in range(1, tensor_n):
-            origin = lax.rem(k - d + tensor_n, tensor_n)
-            remote(
-                x.at[h, k], x.at[h, origin], x_send.at[h, d - 1], x_recv.at[h, d - 1], peer(d)
-            ).wait_recv()
+        for d in range(1, chips):
+            origin = chip_before(d) * 2 + core
+            remote(*block(h, origin, d, across(d))).wait_recv()
+            send(*block(h, origin, chips - 1 + d, sibling))
+    for h in range(2):
+        remote(*block(h, chip * 2 + 1 - core, 0, sibling)).wait_recv()
+        for d in range(1, chips):
+            origin = chip_before(d) * 2 + 1 - core
+            remote(*block(h, origin, chips - 1 + d, sibling)).wait_recv()
     remote(slots_own, slots_far, far_send.at[1], far_recv.at[1], far).wait_recv()
 
     base = (half * (pair_n * (stored_rows // rank_n))).astype(jnp.float32)
@@ -218,9 +271,9 @@
     weights[1].wait()
 
     def project(cols):
-        block = x[...].reshape(toks, width)
-        pre_g[:, cols] = mm(block, wg[cols, :], NT)
-        pre_u[:, cols] = mm(block, wu[cols, :], NT)
+        taken = x[...].reshape(toks, width)
+        pre_g[:, cols] = mm(taken, wg[cols, :], NT)
+        pre_u[:, cols] = mm(taken, wu[cols, :], NT)
 
     tiles(hidden_local, project)
 
@@ -252,35 +305,60 @@
     tiles(hidden_local, activate)
 
     wait_pair(4)
+    own_copies[last].wait()
+    for d in range(1, pair_n):
+        origin = lax.rem(place - d + pair_n, pair_n)
+        remote(*half_of(origin, d, own_share)).wait_recv()
+        send(*handed(origin, d, own_share))
     low = mm(hidden[...], da[...].reshape(rows, hidden_local), NT)
     col_slot = (lax.broadcasted_iota(jnp.int32, (toks, rows), 1) // rank_n).astype(jnp.float32)
     low = jnp.where(slot_cols == col_slot, adapter_scale * low, 0.0).astype(jnp.bfloat16)
-    wait_pair(5)
+    for d in range(1, pair_n):
+        origin = lax.rem(place - d + pair_n, pair_n)
+        remote(*handed(origin, d, other_share)).wait_recv()
     weights[2].wait()
+
+    def to_sibling(c):
+        cols = pl.ds(c * chunk, chunk)
+        return (
+            y.at[:, :, 1 - core, :, cols],
+            y_pair.at[:, :, :, cols],
+            pair_send.at[c],
+            pair_recv.at[c],
+            sibling,
+        )
+
+    def to_chip(c, d):
+        cols = pl.ds(c * chunk, chunk)
+        return (
+            y_sum.at[:, chip_after(d), :, cols],
+            y_in.at[d - 1, :, :, cols],
+            y_send.at[c, d - 1],
+            y_recv.at[c, d - 1],
+            across(d),
+        )
+
+    def join(c):
+        cols = pl.ds(c * chunk, chunk)
+        remote(*to_sibling(c)).wait_recv()
+        both = y[:, :, core, :, cols].astype(jnp.float32) + y_pair[:, :, :, cols].astype(jnp.float32)
+        y_sum[:, :, :, cols] = both.astype(jnp.bfloat16)
+        for d in range(1, chips):
+            send(*to_chip(c, d))
+
     for c in range(SUM_CHUNKS):
         cols = pl.ds(c * chunk, chunk)
         part = mm(hidden[...], wd[:, cols], NN) + mm(low, db[:, :, cols].reshape(rows, chunk), NN)
-        y[:, :, :, cols] = part.astype(jnp.bfloat16).reshape(2, tensor_n, tok_dev, chunk)
-        for d in range(1, tensor_n):
-            to = lax.rem(k + d, tensor_n)
-            send(
-                y.at[:, to, :, cols],
-                y_in.at[d - 1, :, :, cols],
-                y_send.at[c, d - 1],
-                y_recv.at[c, d - 1],
-                peer(d),
-            )
+        y[:, :, :, :, cols] = part.astype(jnp.bfloat16).reshape(2, chips, 2, tok_dev, chunk)
+        send(*to_sibling(c))
+        if c:
+            join(c - 1)
+    join(SUM_CHUNKS - 1)
     for c in range(SUM_CHUNKS):
         cols = pl.ds(c * chunk, chunk)
-        total = y[:, k, :, cols].astype(jnp.float32)
-        for d in range(1, tensor_n):
-            remote(
-                y.at[:, k, :, cols],
-                y_in.at[d - 1, :, :, cols],
-                y_send.at[c, d - 1],
-                y_recv.at[c, d - 1],
-                peer(d),
-            ).wait_recv()
+        total = y_sum[:, chip, :, cols].astype(jnp.float32)
+        for d in range(1, chips):
+            remote(*to_chip(c, d)).wait_recv()
             total = total + y_in[d - 1, :, :, cols].astype(jnp.float32)
         z_out[c] = total[1].astype(jnp.bfloat16)
         send(z_out.at[c], z_in.at[c], far_send.at[2 + c], far_recv.at[2 + c], far)
@@ -354,8 +432,10 @@
             pltpu.VMEM((toks, hidden_local), jnp.float32),
             pltpu.VMEM((toks, hidden_local), jnp.float32),
             pltpu.VMEM((toks, hidden_local), bf),
-            pltpu.VMEM((2, tensor_n, tok_dev, width), bf),
-            pltpu.VMEM((tensor_n - 1, 2, tok_dev, width), bf),
+            pltpu.VMEM((2, tensor_n // 2, 2, tok_dev, width), bf),
+            pltpu.VMEM((2, tensor_n // 2, tok_dev, width), bf),
+            pltpu.VMEM((2, tensor_n // 2, tok_dev, width), bf),
+            pltpu.VMEM((tensor_n // 2 - 1, 2, tok_dev, width), bf),
             pltpu.VMEM((SUM_CHUNKS, tok_dev, chunk), bf),
             pltpu.VMEM((SUM_CHUNKS, tok_dev, chunk), bf),
             pltpu.VMEM((tok_dev, width), jnp.float32),
@@ -365,12 +445,14 @@
             dma((2, tensor_n - 1)),
             dma((2 + SUM_CHUNKS,)),
             dma((2 + SUM_CHUNKS,)),
-            dma((6, max(1, pair_n - 1))),
-            dma((6, max(1, pair_n - 1))),
+            dma((7, max(1, pair_n - 1))),
+            dma((7, max(1, pair_n - 1))),
             dma((tensor_n - 1,)),
             dma((tensor_n - 1,)),
-            dma((SUM_CHUNKS, tensor_n - 1)),
-            dma((SUM_CHUNKS, tensor_n - 1)),
+            dma((SUM_CHUNKS, tensor_n // 2 - 1)),
+            dma((SUM_CHUNKS, tensor_n // 2 - 1)),
+            dma((SUM_CHUNKS,)),
+            dma((SUM_CHUNKS,)),
         ],
         compiler_params=pltpu.CompilerParams(
             collective_id=0, has_side_effects=True, vmem_limit_bytes=60 * 2**20

time: 51.1 us -> 45.7 us (0.89)
  Pallas kernels: 48.1 us -> 42.7 us
    pallas_call x1, Pallas kernels: 48.1 us -> 42.7 us  [local(): pl.pallas_call(functools.partial(kernel, tensor_n, pair_n), out_shape=jax...]
where the time goes in v2:
time: 45.7 us; the launch traced here: 45.4 us
  Pallas kernels  42.7 us (93%)
  local copies, waits for them, and re-layouts  2.76 us (6%)
    pallas_call x1, Pallas kernels, local(): pl.pallas_call(functools.partial(kernel, tensor_n, pair_n), out_shape=jax...  42.7 us
    unnamed x1, local copies, waits for them, and re-layouts  1.47 us
    broadcast_in_dim x1, local copies, waits for them, and re-layouts, local(): norm_gain[None]  1.29 us

profile of v2, /device:TPU:0, one launch (start us, length us, event | category | flops | bytes accessed | tf_op | source)
XLA Modules:
  0.0 45.4 jit_solution(453110044163762800)
XLA Ops:
  0.0 1.3 %broadcast_in_dim.6.gain_ref = bf16[1,2048]{1,0:T(2,128)(2,1)} reshape(bf16[2048]{0:T(1024)(128)(2,1)} %param.16) | data formatting | bytes 8192 | tf_op jit(solution)/shard_map/broadcast_in_dim | solution.py:463
  1.3 42.7 %ffn.1 = bf16[16,2048]{1,0:T(8,128)(2,1)} custom-call(bf16[16,2048]{1,0:T(8,128)(2,1)} %bitcast.23, bf16[1,2048]{1,0:T(2,128)(2,1)} %broadcast_in_dim.6.gain_ref, bf16[1368,2048]{1,0:T(8,128)(2,1)} %bitcast.16, bf16[1368,2048]{1,0:T(8,128)(2,1)} %bitcast.17, bf16[1368,2048]{1,0:T(8,128)(2,1)} %wd_hbm.1, bf16[64,256]{1,0:T(8,128)(2,1)} %bitcast.24, ...), custom_call_target="tpu_custom_call" | custom-call | tf_op jit(solution)/shard_map/ffn/pallas_call | solution.py:412
  44.0 1.5 %copy.17 = bf16[1,16,2048]{2,1,0:T(8,128)(2,1)} copy(bf16[1,16,2048]{2,1,0:T(8,128)(2,1)} %bitcast.19) | data formatting | bytes 131072
